TPU v7x, 256 devices: a whole 4x4x8 slice. The times are simulated.
256 devices in a mesh: dp: 4 (over y), blk: 32 (over z_lo, x, core), uly: 2 (over z_hi).
Axes of the slice: x: 4, y: 4, z: 8 (z_hi: 2, z_lo: 4; z = z_hi * 4 + z_lo), core: 2. Of those that a mesh axis runs over, the one named last changes fastest.
Arguments:
- queries: bfloat16 [16384, 2560], P(('dp', 'blk', 'uly')), parts along dimension 0, may hold values from -8 to 8, as said below
- keys: bfloat16 [16384, 2560], P(('dp', 'blk', 'uly')), parts along dimension 0, may hold values from -8 to 8, as said below
- values: bfloat16 [16384, 2560], P(('dp', 'blk', 'uly')), parts along dimension 0, may hold values from -6 to 6
- query_tangent: bfloat16 [16384, 2560], P(('dp', 'blk', 'uly')), parts along dimension 0, may hold values from -6 to 6
- key_tangent: bfloat16 [16384, 2560], P(('dp', 'blk', 'uly')), parts along dimension 0, may hold values from -6 to 6
- value_tangent: bfloat16 [16384, 2560], P(('dp', 'blk', 'uly')), parts along dimension 0, may hold values from -6 to 6
Outputs:
- attended: bfloat16 [16384, 2560], P(('dp', 'blk', 'uly')), parts along dimension 0
- attended_tangent: bfloat16 [16384, 2560], P(('dp', 'blk', 'uly')), parts along dimension 0
There are 4 independent parts, one for each index of `dp`. A program takes and returns all parts, laid end to end along the dimension named above; each array names one. Nothing has to cross between parts.
Inputs may be any that keep to these rules, and one draw needn't show every extreme that they name: `queries`: entries are real numbers of order one. `keys`: entries are real numbers of order one.
All inputs are finite; a program needn't handle non-finite values.
Results may differ from a plain program's by a relative error of at most 0.015.
Values may be sent and summed in bfloat16 or wider, within the bound.
A program may use at most 256 MiB of HBM per device.

v0:
```python
import jax
import jax.numpy as jnp
from jax import lax
from jax.sharding import PartitionSpec as P

HEADS = 20


floor_value = -1e30


def head_major(block, n_heads):
    return jnp.moveaxis(block.reshape(block.shape[0], n_heads, block.shape[1] // n_heads), 1, 0)


def token_major(block):
    return jnp.moveaxis(block, 0, 1).reshape(block.shape[1], block.shape[0] * block.shape[2])


def scores_of(query_part, key_part):
    return jnp.einsum("qd,kd->qk", query_part, key_part, preferred_element_type=jnp.float32)


def make_start(n_heads, q_rows, head_width):
    start_best = jnp.full((n_heads, q_rows), floor_value, jnp.float32)
    zero_rows = jnp.zeros((n_heads, q_rows), jnp.float32)
    zero_accum = jnp.zeros((n_heads, q_rows, head_width), jnp.float32)
    return (start_best, zero_rows, zero_rows, zero_accum, zero_accum)


def make_step(query_heads, qdot_heads, n_heads, state_in, block_in):
    score_scale = query_heads.shape[2] ** (-0.5)
    key_blk, kdot_blk, value_blk, vdot_blk = (head_major(member, n_heads) for member in block_in)

    def per_head(per_items):
        (
            query_one,
            qdot_one,
            key_one,
            kdot_one,
            value_one,
            vdot_one,
            best_old,
            total_old,
            tilt_old,
            accum_old,
            tacc_old,
        ) = per_items
        scores = scores_of(query_one, key_one) * score_scale
        score_dot = (scores_of(qdot_one, key_one) + scores_of(query_one, kdot_one)) * score_scale
        best_new = jnp.maximum(best_old, jnp.max(scores, axis=1))
        shrink_by = jnp.exp(best_old - best_new)
        expo_vals = jnp.exp(scores - best_new[:, None])
        weighted = expo_vals * score_dot
        probs_low = expo_vals.astype(jnp.bfloat16)
        weigh_low = weighted.astype(jnp.bfloat16)
        total_new = total_old * shrink_by + jnp.sum(expo_vals, axis=1)
        tilt_new = tilt_old * shrink_by + jnp.sum(weighted, axis=1)
        accum_new = accum_old * shrink_by[:, None] + jnp.dot(
            probs_low, value_one, preferred_element_type=jnp.float32
        )
        tacc_new = (
            tacc_old * shrink_by[:, None]
            + jnp.dot(weigh_low, value_one, preferred_element_type=jnp.float32)
            + jnp.dot(probs_low, vdot_one, preferred_element_type=jnp.float32)
        )
        return (best_new, total_new, tilt_new, accum_new, tacc_new)

    return lax.map(
        per_head,
        (query_heads, qdot_heads, key_blk, kdot_blk, value_blk, vdot_blk) + tuple(state_in),
    )


def finish(state_out):
    best_row, totals, tilt, primal_sum, tangent_sum = state_out
    output = primal_sum / totals[:, :, None]
    tangent = tangent_sum / totals[:, :, None] - output * (tilt / totals)[:, :, None]
    return (token_major(output.astype(jnp.bfloat16)), token_major(tangent.astype(jnp.bfloat16)))


def shards(queries, keys, values, query_tangent, key_tangent, value_tangent):
    n_heads = HEADS // lax.axis_size("uly")
    exchanged = (
        lax.all_to_all(queries, "uly", split_axis=1, concat_axis=0, tiled=True),
        lax.all_to_all(query_tangent, "uly", split_axis=1, concat_axis=0, tiled=True),
        lax.all_to_all(keys, "uly", split_axis=1, concat_axis=0, tiled=True),
        lax.all_to_all(key_tangent, "uly", split_axis=1, concat_axis=0, tiled=True),
        lax.all_to_all(values, "uly", split_axis=1, concat_axis=0, tiled=True),
        lax.all_to_all(value_tangent, "uly", split_axis=1, concat_axis=0, tiled=True),
    )
    query_all, qdot_all, key_local, kdot_local, value_local, vdot_local = exchanged
    query_heads = head_major(query_all, n_heads)
    qdot_heads = head_major(qdot_all, n_heads)
    start = make_start(n_heads, query_heads.shape[1], query_heads.shape[2])
    state_out = make_step(
        query_heads,
        qdot_heads,
        n_heads,
        start,
        (
            lax.all_gather(key_local, "blk", axis=0, tiled=True),
            lax.all_gather(kdot_local, "blk", axis=0, tiled=True),
            lax.all_gather(value_local, "blk", axis=0, tiled=True),
            lax.all_gather(vdot_local, "blk", axis=0, tiled=True),
        ),
    )
    output_tok, tangent_tok = finish(state_out)
    attended, attended_tangent = (
        lax.all_to_all(output_tok, "uly", split_axis=0, concat_axis=1, tiled=True),
        lax.all_to_all(tangent_tok, "uly", split_axis=0, concat_axis=1, tiled=True),
    )
    return (attended, attended_tangent)


def solution(mesh):
    in_specs = (
        P(("dp", "blk", "uly"), None),
        P(("dp", "blk", "uly"), None),
        P(("dp", "blk", "uly"), None),
        P(("dp", "blk", "uly"), None),
        P(("dp", "blk", "uly"), None),
        P(("dp", "blk", "uly"), None),
    )
    out_specs = (P(("dp", "blk", "uly"), None), P(("dp", "blk", "uly"), None))
    return jax.shard_map(shards, mesh=mesh, in_specs=in_specs, out_specs=out_specs, check_vma=False)
```

profile of v0, /device:TPU:16, one launch (start us, length us, event | category | flops | bytes accessed | tf_op | source)
XLA Modules:
  0.0 518.3 jit_solution(15793150675327511301)
XLA Ops:
  8.3 20.9 %all_to_all.146 = bf16[64,2,1280]{2,0,1:T(8,128)(2,1)} all-to-all(bf16[64,2,1280]{2,0,1:T(8,128)(2,1)S(1)} %bitcast.155), channel_id=1, replica_groups=mesh['dp'=4,'blk'=32,'uly'=2] {'uly'}, dimensions={1} | all-to-all | bytes 655360 | tf_op jit(solution)/shard_map/all_to_all | solution.py:87
  30.2 14.5 %all_to_all.147 = bf16[64,2,1280]{2,0,1:T(8,128)(2,1)} all-to-all(bf16[64,2,1280]{2,0,1:T(8,128)(2,1)S(1)} %bitcast.156), channel_id=1, replica_groups=mesh['dp'=4,'blk'=32,'uly'=2] {'uly'}, dimensions={1} | all-to-all | bytes 655360 | tf_op jit(solution)/shard_map/all_to_all | solution.py:88
  44.9 18.0 %all_to_all.148 = bf16[64,2,1280]{2,0,1:T(8,128)(2,1)} all-to-all(bf16[64,2,1280]{2,0,1:T(8,128)(2,1)S(1)} %bitcast.157), channel_id=1, replica_groups=mesh['dp'=4,'blk'=32,'uly'=2] {'uly'}, dimensions={1} | all-to-all | bytes 655360 | tf_op jit(solution)/shard_map/all_to_all | solution.py:89
  63.0 17.7 %all_to_all.149 = bf16[64,2,1280]{2,0,1:T(8,128)(2,1)} all-to-all(bf16[64,2,1280]{2,0,1:T(8,128)(2,1)S(1)} %bitcast.158), channel_id=1, replica_groups=mesh['dp'=4,'blk'=32,'uly'=2] {'uly'}, dimensions={1} | all-to-all | bytes 655360 | tf_op jit(solution)/shard_map/all_to_all | solution.py:90
  81.5 3.5 all-to-all-start
  85.8 13.9 %all-to-all-done = bf16[64,2,1280]{2,0,1:T(8,128)(2,1)S(1)} async-done(((bf16[64,2,1280]{2,0,1:T(8,128)(2,1)}), bf16[64,2,1280]{2,0,1:T(8,128)(2,1)S(1)}, u32[]{:S(2)}, u32[]{:S(2)}) %all-to-all-start) | async-done | bytes 327712 | tf_op jit(solution)/shard_map/all_to_all | solution.py:85
  99.7 3.5 all-to-all-start.2
  103.5 14.1 %all-to-all-done.2 = bf16[64,2,1280]{2,0,1:T(8,128)(2,1)S(1)} async-done(((bf16[64,2,1280]{2,0,1:T(8,128)(2,1)}), bf16[64,2,1280]{2,0,1:T(8,128)(2,1)S(1)}, u32[]{:S(2)}, u32[]{:S(2)}) %all-to-all-start.2) | async-done | bytes 327712 | tf_op jit(solution)/shard_map/all_to_all | solution.py:86
  117.9 8.9 %all-gather.5.cloned.1.call-done = bf16[4096,1280]{1,0:T(8,128)(2,1)} async-done(((bf16[128,1280]{1,0:T(8,128)(2,1)}), bf16[4096,1280]{1,0:T(8,128)(2,1)}) %all-gather.5.cloned.1.call-update) | async-done | bytes 10485776 | tf_op jit(solution)/shard_map/all_gather | solution.py:102
  126.8 14.3 %copy.44 = bf16[4096,1280]{0,1:T(8,128)(2,1)} copy(bf16[4096,1280]{1,0:T(8,128)(2,1)} %all-gather.5.cloned.1.call-done) | data formatting | bytes 20971520 | tf_op jit(solution)/shard_map/all_gather | solution.py:102
  141.1 59.7 %all-gather.7.cloned.1.call-done = bf16[4096,1280]{1,0:T(8,128)(2,1)} async-done(((bf16[128,1280]{1,0:T(8,128)(2,1)}), bf16[4096,1280]{1,0:T(8,128)(2,1)}) %all-gather.7.cloned.1.call-update) | async-done | bytes 10485776 | tf_op jit(solution)/shard_map/all_gather | solution.py:103
  200.8 14.4 %copy.47 = bf16[4096,1280]{0,1:T(8,128)(2,1)} copy(bf16[4096,1280]{1,0:T(8,128)(2,1)} %all-gather.7.cloned.1.call-done) | data formatting | bytes 20971520 | tf_op jit(solution)/shard_map/all_gather | solution.py:103
  215.2 58.9 %all-gather.9.cloned.1.call-done = bf16[4096,1280]{1,0:T(8,128)(2,1)} async-done(((bf16[128,1280]{1,0:T(8,128)(2,1)}), bf16[4096,1280]{1,0:T(8,128)(2,1)}) %all-gather.9.cloned.1.call-update) | async-done | bytes 10485776 | tf_op jit(solution)/shard_map/all_gather | solution.py:104
  274.1 14.3 %copy.49 = bf16[4096,1280]{0,1:T(8,128)(2,1)} copy(bf16[4096,1280]{1,0:T(8,128)(2,1)} %all-gather.9.cloned.1.call-done) | data formatting | bytes 20971520 | tf_op jit(solution)/shard_map/all_gather | solution.py:104
  288.4 58.8 %all-gather.11.cloned.1.call-done = bf16[4096,1280]{1,0:T(8,128)(2,1)} async-done(((bf16[128,1280]{1,0:T(8,128)(2,1)}), bf16[4096,1280]{1,0:T(8,128)(2,1)}) %all-gather.11.cloned.1.call-update) | async-done | bytes 10485776 | tf_op jit(solution)/shard_map/all_gather | solution.py:105
  347.2 14.3 %copy.51 = bf16[4096,1280]{0,1:T(8,128)(2,1)} copy(bf16[4096,1280]{1,0:T(8,128)(2,1)} %all-gather.11.cloned.1.call-done) | data formatting | bytes 20971520 | tf_op jit(solution)/shard_map/all_gather | solution.py:105
  361.5 114.9 %while.16 = (s32[]{:T(128)}, f32[10,128]{1,0:T(8,128)S(1)}, f32[10,128]{1,0:T(8,128)S(1)}, f32[10,128,128]{2,1,0:T(8,128)S(1)}, f32[10,128,128]{2,1,0:T(8,128)S(...) while((s32[]{:T(128)}, f32[10,128]{1,0:T(8,128)S(1)}, ...), condition=%wide.region_4.5_spmd, body=%wide.region_0.4_spmd.sunk | while | flops 812695936 | bytes 23446148 | solution.py:69
  361.5 1.7 fusion.63
  364.9 2.1 fusion.64
  368.8 1.8 fusion.67
  370.6 1.8 fusion.66
  373.0 1.7 fusion.63
  376.4 2.1 fusion.64
  378.5 1.7 convolution_add_fusion.5
  380.3 1.8 fusion.67
  382.1 1.8 fusion.66
  384.5 1.7 fusion.63
  387.9 2.1 fusion.64
  391.7 1.8 fusion.67
  393.6 1.8 fusion.66
  396.0 1.7 fusion.63
  399.4 2.1 fusion.64
  401.5 1.7 convolution_add_fusion.5
  403.2 1.8 fusion.67
  405.1 1.8 fusion.66
  407.5 1.7 fusion.63
  410.9 2.1 fusion.64
  414.7 1.8 fusion.67
  416.6 1.8 fusion.66
  419.0 1.7 fusion.63
  422.4 2.1 fusion.64
  424.5 1.7 convolution_add_fusion.5
  426.2 1.8 fusion.67
  428.1 1.8 fusion.66
  430.4 1.7 fusion.63
  433.8 2.1 fusion.64
  437.7 1.8 fusion.67
  439.6 1.8 fusion.66
  441.9 1.7 fusion.63
  445.3 2.1 fusion.64
  449.2 1.8 fusion.67
  451.0 1.8 fusion.66
  453.4 1.7 fusion.63
  456.8 2.1 fusion.64
  460.7 1.8 fusion.67
  462.5 1.8 fusion.66
  464.9 1.7 fusion.63
  468.3 2.1 fusion.64
  472.2 1.8 fusion.67
  474.0 1.8 fusion.66
  478.0 5.6 %all-to-all-start.6 = ((bf16[2,64,1280]{2,1,0:T(8,128)(2,1)}), bf16[2,64,1280]{2,1,0:T(8,128)(2,1)S(1)}, u32[]{:S(2)}, u32[]{:S(2)}) async-start(bf16[2,64,1280]{2,1,0:T(8,128)(2,1)} %all_to_all.130), calls=%async_computation.6 | async-start | bytes 655360 | tf_op jit(solution)/shard_map/all_to_all | solution.py:110
  484.8 11.5 %all-to-all-done.6 = bf16[2,64,1280]{2,1,0:T(8,128)(2,1)S(1)} async-done(((bf16[2,64,1280]{2,1,0:T(8,128)(2,1)}), bf16[2,64,1280]{2,1,0:T(8,128)(2,1)S(1)}, u32[]{:S(2)}, u32[]{:S(2)}) %all-to-all-start.6) | async-done | bytes 327712 | tf_op jit(solution)/shard_map/all_to_all | solution.py:110
  496.3 3.5 all-to-all-start.7
  500.5 10.5 %all-to-all-done.7 = bf16[2,64,1280]{2,1,0:T(8,128)(2,1)S(1)} async-done(((bf16[2,64,1280]{2,1,0:T(8,128)(2,1)}), bf16[2,64,1280]{2,1,0:T(8,128)(2,1)S(1)}, u32[]{:S(2)}, u32[]{:S(2)}) %all-to-all-start.7) | async-done | bytes 327712 | tf_op jit(solution)/shard_map/all_to_all | solution.py:111
  (115 shorter events, 42.5 us)
Async XLA Ops:
  7.2 37.7 %copy-start = (bf16[64,2560]{1,0:T(8,128)(2,1)S(1)}, bf16[64,2560]{1,0:T(8,128)(2,1)}, u32[]{:S(2)}) copy-start(bf16[64,2560]{1,0:T(8,128)(2,1)} %param.10) | copy-start | bytes 983044
  7.2 119.6 %all-gather.5.cloned.1.call-start = ((), (), s32[]{:S(2)}) async-start(), calls=%async_computation.8 | async-start | bytes 10813440 | tf_op jit(solution)/shard_map/all_gather | solution.py:102
  8.3 54.7 %copy-start.1 = (bf16[64,2560]{1,0:T(8,128)(2,1)S(1)}, bf16[64,2560]{1,0:T(8,128)(2,1)}, u32[]{:S(2)}) copy-start(bf16[64,2560]{1,0:T(8,128)(2,1)} %param.13) | copy-start | bytes 983044
  29.2 171.6 %all-gather.7.cloned.1.call-start = ((), (), s32[]{:S(2)}) async-start(), calls=%async_computation.9 | async-start | bytes 10813440 | tf_op jit(solution)/shard_map/all_gather | solution.py:103
  30.2 50.5 %copy-start.2 = (bf16[64,2560]{1,0:T(8,128)(2,1)S(1)}, bf16[64,2560]{1,0:T(8,128)(2,1)}, u32[]{:S(2)}) copy-start(bf16[64,2560]{1,0:T(8,128)(2,1)} %param.8) | copy-start | bytes 983044
  44.8 229.3 %all-gather.9.cloned.1.call-start = ((), (), s32[]{:S(2)}) async-start(), calls=%async_computation.10 | async-start | bytes 10813440 | tf_op jit(solution)/shard_map/all_gather | solution.py:104
  44.9 40.1 %copy-start.3 = (bf16[64,2560]{1,0:T(8,128)(2,1)S(1)}, bf16[64,2560]{1,0:T(8,128)(2,1)}, u32[]{:S(2)}) copy-start(bf16[64,2560]{1,0:T(8,128)(2,1)} %param.11) | copy-start | bytes 983044
  62.9 284.3 %all-gather.11.cloned.1.call-start = ((), (), s32[]{:S(2)}) async-start(), calls=%async_computation.11 | async-start | bytes 10813440 | tf_op jit(solution)/shard_map/all_gather | solution.py:105
  81.5 18.1 %all-to-all-start = ((bf16[64,2,1280]{2,0,1:T(8,128)(2,1)}), bf16[64,2,1280]{2,0,1:T(8,128)(2,1)S(1)}, u32[]{:S(2)}, u32[]{:S(2)}) async-start(bf16[64,2,1280]{2,0,1:T(8,128)(2,1)} %bitcast.112), calls=%async_computation | async-start | bytes 655360 | tf_op jit(solution)/shard_map/all_to_all | solution.py:85
  99.7 18.0 %all-to-all-start.2 = ((bf16[64,2,1280]{2,0,1:T(8,128)(2,1)}), bf16[64,2,1280]{2,0,1:T(8,128)(2,1)S(1)}, u32[]{:S(2)}, u32[]{:S(2)}) async-start(bf16[64,2,1280]{2,0,1:T(8,128)(2,1)} %bitcast.110), calls=%async_computation.2 | async-start | bytes 655360 | tf_op jit(solution)/shard_map/all_to_all | solution.py:86
  478.0 18.3 %all-to-all-start.6 = ((bf16[2,64,1280]{2,1,0:T(8,128)(2,1)}), bf16[2,64,1280]{2,1,0:T(8,128)(2,1)S(1)}, u32[]{:S(2)}, u32[]{:S(2)}) async-start(bf16[2,64,1280]{2,1,0:T(8,128)(2,1)} %all_to_all.130), calls=%async_computation.6 | async-start | bytes 655360 | tf_op jit(solution)/shard_map/all_to_all | solution.py:110
  496.3 14.7 %all-to-all-start.7 = ((bf16[2,64,1280]{2,1,0:T(8,128)(2,1)}), bf16[2,64,1280]{2,1,0:T(8,128)(2,1)S(1)}, u32[]{:S(2)}, u32[]{:S(2)}) async-start(bf16[2,64,1280]{2,1,0:T(8,128)(2,1)} %all_to_all.134), calls=%async_computation.7 | async-start | bytes 655360 | tf_op jit(solution)/shard_map/all_to_all | solution.py:111
Sparse Core Ops, SparseCore 0:
  29.3 97.4 all-gather.4
  128.7 72.0 all-gather.6
  202.6 71.3 all-gather.8
  275.8 71.4 all-gather.10
where the time goes:
time: 522 us; the launch traced here: 518 us
  waiting for transfers between devices  236 us (45%)
  matrix products  109 us (21%)
  blocking collectives  71.2 us (14%)
  local copies, waits for them, and re-layouts  66 us (13%)
  starting transfers between devices  16.1 us (3%)
  between operations  14 us (3%)
    all_gather x1, waiting for transfers between devices, shards(): lax.all_gather(kdot_local, 'blk', axis=0, tiled=True)  59.7 us
    all_gather x1, waiting for transfers between devices, shards(): lax.all_gather(value_local, 'blk', axis=0, tiled=True)  58.9 us
    all_gather x1, waiting for transfers between devices, shards(): lax.all_gather(vdot_local, 'blk', axis=0, tiled=True)  58.8 us
    dot_general x30, matrix products, scores_of(): jnp.einsum('qd,kd->qk', query_part, key_part, preferred_element_type=jnp....  55.1 us
    all_to_all x1, blocking collectives, shards(): lax.all_to_all(keys, 'uly', split_axis=1, concat_axis=0, tiled=True)  20.9 us
    dot_general x10, matrix products, per_head(): jnp.dot(probs_low, value_one, preferred_element_type=jnp.float32)  18.4 us
    dot_general x10, matrix products, per_head(): jnp.dot(probs_low, vdot_one, preferred_element_type=jnp.float32)  18.4 us
    all_to_all x1, blocking collectives, shards(): lax.all_to_all(values, 'uly', split_axis=1, concat_axis=0, tiled=True)  18 us
  transfers between devices with their start and end apart: 8, of which 8 were waited for; matrix products, arithmetic and copies ran while one was open for 9% of the time, Pallas kernels for 0%

commit v1 on v0

v1 whole, which is shorter than its diff:
```python
import functools
import math

import jax
import jax.numpy as jnp
from jax import lax
from jax.experimental import pallas as pl
from jax.experimental.pallas import tpu as pltpu
from jax.sharding import PartitionSpec as P

HEADS = 20
HD = 128
TOK = 64
NZ, NX, NC = 8, 4, 2
KEYS = TOK * NX * NC
QROWS = TOK * NZ
SLOTS = 3
SCALE = HD ** -0.5
TO_LOG2 = SCALE * math.log2(math.e)
LAG_X, LAG_RELAY, LAG_COMPUTE = 2, 4, 6


def head_of(z, slot):
    base = 5 * (z // 2)
    if slot == 0:
        return base + 2
    return base + 3 * lax.rem(z, 2) + (slot - 1)


def head_dyn(z, slot):
    base = 5 * (z // 2)
    return base + jnp.where(slot == 0, 2, 3 * lax.rem(z, 2) + slot - 1)


def dot_t(a, b):
    return lax.dot_general(a, b, (((1,), (1,)), ((), ())), preferred_element_type=jnp.float32)


def dot(a, b):
    return lax.dot_general(a, b, (((1,), (0,)), ((), ())), preferred_element_type=jnp.float32)


def attend(q, kv, m_ref, l_ref, ap_ref, aw_ref):
    s = dot_t(q[:, HD:], kv[:, :HD])
    sd = dot_t(q[:, :], kv[:, : 2 * HD])
    n = s.shape[1]
    best = s[:, :HD]
    for j in range(HD, n, HD):
        best = jnp.maximum(best, s[:, j : j + HD])
    best = jnp.max(best, axis=1, keepdims=True) * TO_LOG2
    m_old = m_ref[...]
    m_new = jnp.maximum(m_old, jnp.broadcast_to(best, m_old.shape))
    alpha = jnp.exp2(m_old - m_new)
    m_ref[...] = m_new
    p = jnp.exp2(s * TO_LOG2 - jnp.concatenate([m_new] * (n // HD), axis=1))
    w = p * sd
    total = p[:, :HD]
    for j in range(HD, n, HD):
        total = total + p[:, j : j + HD]
    v = kv[:, 3 * HD :]
    po = dot(p.astype(jnp.bfloat16), kv[:, 2 * HD :])
    wo = dot(w.astype(jnp.bfloat16), jnp.concatenate([v, jnp.ones_like(v)], axis=1))
    alpha2 = jnp.concatenate([alpha, alpha], axis=1)
    l_ref[...] = l_ref[...] * alpha + total
    ap_ref[...] = ap_ref[...] * alpha2 + po
    aw_ref[...] = aw_ref[...] * alpha2 + wo


def kernel(
    q_hbm, k_hbm, v_hbm, qd_hbm, kd_hbm, vd_hbm, o_ref, t_ref,
    stage, pack_kv, pack_q, kv, qb, ob, m_ref, l_ref, ap_ref, aw_ref,
    load_sem, zkv_s, zkv_r, zq_s, zq_r, x_s, x_r, rel_s, rel_r, sib_s, sib_r, out_s, out_r,
):
    blk, uly = lax.axis_index("blk"), lax.axis_index("uly")
    core = lax.rem(blk, NC)
    x = lax.rem(blk // NC, NX)
    z = uly * 4 + blk // (NC * NX)
    even = lax.rem(z, 2) == 0

    def device(zz, xx, cc):
        return {"blk": (lax.rem(zz, 4) * NX + xx) * NC + cc, "uly": zz // 4}

    def z_peer(dz):
        return lax.rem(z + dz, NZ)

    def x_peer(dx):
        return lax.rem(x + dx, NX)

    other = 1 - core
    sibling = device(z, x, other)
    right, left = device(z, x_peer(1), core), device(z, x_peer(3), core)

    def remote(src, dst, send, recv, to):
        return pltpu.make_async_remote_copy(
            src_ref=src, dst_ref=dst, send_sem=send, recv_sem=recv,
            device_id=to, device_id_type=pl.DeviceIdType.MESH,
        )

    barrier = pltpu.get_barrier_semaphore()
    for dz in range(1, NZ):
        pl.semaphore_signal(barrier, inc=1, device_id=device(z_peer(dz), x, core), device_id_type=pl.DeviceIdType.MESH)
    for to in (sibling, right, left):
        pl.semaphore_signal(barrier, inc=1, device_id=to, device_id_type=pl.DeviceIdType.MESH)

    loads = []
    for i, ref in enumerate((k_hbm, kd_hbm, vd_hbm, v_hbm, qd_hbm, q_hbm)):
        copy = pltpu.make_async_copy(ref, stage.at[i], load_sem.at[i])
        copy.start()
        loads.append(copy)
    for copy in loads:
        copy.wait()

    def pack(h):
        columns = pl.ds(h * HD, HD)
        for i in range(4):
            pack_kv[h, :, i * HD : (i + 1) * HD] = stage[i, :, columns]
        for i in range(2):
            pack_q[h, :, i * HD : (i + 1) * HD] = stage[4 + i, :, columns]

    for h in range(HEADS):
        pack(h)

    def place(xx, cc):
        return pl.ds(pl.multiple_of((xx * NC + cc) * TOK, TOK), TOK)

    mine = place(x, core)
    my_rows = pl.ds(pl.multiple_of(z * TOK, TOK), TOK)

    def own(slot):
        h = head_of(z, slot)
        kv[slot, z, mine, :] = pack_kv[h]
        qb[slot, my_rows, :] = pack_q[h]

    pl.when(even)(lambda: own(0))
    own(1)
    own(2)

    pl.semaphore_wait(barrier, NZ - 1 + 3)

    def send_kv(slot, dz):
        zz = z_peer(dz)
        remote(pack_kv.at[head_of(zz, slot)], kv.at[slot, z, mine], zkv_s.at[slot], zkv_r.at[slot, dz],
               device(zz, x, core)).start()

    def send_q(slot, dz):
        zz = z_peer(dz)
        remote(pack_q.at[head_of(zz, slot)], qb.at[slot, my_rows], zq_s.at[slot], zq_r.at[slot],
               device(zz, x, core)).start()

    def send_all(slot, send):
        for dz in (1, 7, 2, 6, 3, 5, 4):
            if slot == 0:
                pl.when(lax.rem(z + dz, 2) == 0)(functools.partial(send, slot, dz))
            else:
                send(slot, dz)

    send_all(0, send_kv)
    send_all(0, send_q)
    send_all(1, send_kv)
    send_all(1, send_q)
    send_all(2, send_q)
    send_all(2, send_kv)

    toward = jnp.where(core == 0, 1, 3)
    relay_to = device(z, x_peer(toward), core)
    relay_block = place(x_peer(NX - toward), core)
    left_block, right_block, far_block = place(x_peer(3), core), place(x_peer(1), core), place(x_peer(2), core)

    def unpack_step(n):
        slot, i = n // NZ, lax.rem(n, NZ)
        half = (i + 1) // 2
        dz = jnp.where(lax.rem(i, 2) == 1, half, lax.rem(NZ - half, NZ))
        zz = lax.rem(z - dz + NZ, NZ)
        return slot, i, dz, zz

    def to_sibling(slot, i, zz, block):
        ref = kv.at[slot, zz, block]
        remote(ref, ref, sib_s.at[slot], sib_r.at[slot, i], sibling).start()

    def from_z(n):
        slot, i, dz, zz = unpack_step(n)
        ref = kv.at[slot, zz, mine]

        @pl.when(i > 0)
        def _():
            remote(ref, ref, zkv_s.at[slot], zkv_r.at[slot, dz], right).wait_recv()

        remote(ref, ref, x_s.at[slot], x_r.at[slot, i, 0], right).start()
        remote(ref, ref, x_s.at[slot], x_r.at[slot, i, 1], left).start()
        to_sibling(slot, i, zz, mine)

    def from_x(n):
        slot, i, dz, zz = unpack_step(n)
        l_at, r_at, rel = kv.at[slot, zz, left_block], kv.at[slot, zz, right_block], kv.at[slot, zz, relay_block]
        remote(l_at, l_at, x_s.at[slot], x_r.at[slot, i, 0], right).wait_recv()
        remote(r_at, r_at, x_s.at[slot], x_r.at[slot, i, 1], left).wait_recv()
        remote(rel, rel, rel_s.at[slot], rel_r.at[slot, i], relay_to).start()
        to_sibling(slot, i, zz, left_block)
        to_sibling(slot, i, zz, right_block)

    def from_relay(n):
        slot, i, dz, zz = unpack_step(n)
        far = kv.at[slot, zz, far_block]
        remote(far, far, rel_s.at[slot], rel_r.at[slot, i], relay_to).wait_recv()
        to_sibling(slot, i, zz, far_block)

    def compute(n):
        slot, i, dz, zz = unpack_step(n)
        four = kv.at[slot, zz, pl.ds(0, 4 * TOK)]
        remote(four, four, sib_s.at[slot], sib_r.at[slot, i], sibling).wait_recv()

        @pl.when(i == 0)
        def _():
            seven = qb.at[slot, pl.ds(0, QROWS - TOK)]
            remote(seven, seven, zq_s.at[slot], zq_r.at[slot], right).wait_recv()
            m_ref[...] = jnp.full_like(m_ref, -1e30)
            l_ref[...] = jnp.zeros_like(l_ref)
            ap_ref[...] = jnp.zeros_like(ap_ref)
            aw_ref[...] = jnp.zeros_like(aw_ref)

        attend(qb.at[slot], kv.at[slot, zz], m_ref, l_ref, ap_ref, aw_ref)

        @pl.when(i == NZ - 1)
        def _():
            inv = 1.0 / jnp.sum(l_ref[...], axis=1, keepdims=True)
            o = ap_ref[:, HD:] * inv
            tilt = aw_ref[:, HD:] * (SCALE * inv)
            tangent = (ap_ref[:, :HD] + aw_ref[:, :HD] * SCALE) * inv - o * tilt
            ob[slot, 0] = o.astype(jnp.bfloat16)
            ob[slot, 1] = tangent.astype(jnp.bfloat16)
            columns = pl.ds(pl.multiple_of(head_dyn(z, slot) * HD, HD), HD)
            o_ref[:, columns] = ob[slot, 0, my_rows, :]
            t_ref[:, columns] = ob[slot, 1, my_rows, :]
            for dz in (4, 3, 5, 2, 6, 1, 7):
                to_z = z_peer(dz)
                rows = pl.ds(pl.multiple_of(to_z * TOK, TOK), TOK)
                to = device(to_z, x, core)
                remote(ob.at[slot, 0, rows], o_ref.at[:, columns], out_s.at[slot], out_r.at[0], to).start()
                remote(ob.at[slot, 1, rows], t_ref.at[:, columns], out_s.at[slot], out_r.at[1], to).start()

    first = jnp.where(even, 0, NZ)
    last = SLOTS * NZ

    def step(n, carry):
        for lag, do in ((0, from_z), (LAG_X, from_x), (LAG_RELAY, from_relay), (LAG_COMPUTE, compute)):
            pl.when(jnp.logical_and(n - lag >= first, n - lag < last))(functools.partial(do, n - lag))
        return carry

    lax.fori_loop(first, last + LAG_COMPUTE, step, 0)

    def drain_sends(slot):
        z_kv = pack_kv.at[pl.ds(0, NZ - 1)]
        z_q = pack_q.at[pl.ds(0, NZ - 1)]
        if slot > 0:
            remote(z_kv, z_kv, zkv_s.at[slot], zkv_r.at[slot, 1], right).wait_send()
            remote(z_q, z_q, zq_s.at[slot], zq_r.at[slot], right).wait_send()
        x_all, rel_all, sib_all = kv.at[slot, pl.ds(0, 2)], kv.at[slot, 0], kv.at[slot, pl.ds(0, 4)]
        remote(x_all, x_all, x_s.at[slot], x_r.at[slot, 0, 0], right).wait_send()
        remote(rel_all, rel_all, rel_s.at[slot], rel_r.at[slot, 0], right).wait_send()
        remote(sib_all, sib_all, sib_s.at[slot], sib_r.at[slot, 0], right).wait_send()
        out_all = ob.at[slot, :, pl.ds(0, QROWS - TOK)]
        remote(out_all, out_all, out_s.at[slot], out_r.at[0], right).wait_send()

    pl.when(even)(lambda: drain_sends(0))
    drain_sends(1)
    drain_sends(2)

    def drain_parity(targets, foreign):
        z_kv = pack_kv.at[pl.ds(0, targets)]
        z_q = pack_q.at[pl.ds(0, targets)]
        remote(z_kv, z_kv, zkv_s.at[0], zkv_r.at[0, 1], right).wait_send()
        remote(z_q, z_q, zq_s.at[0], zq_r.at[0], right).wait_send()
        o_all, t_all = o_ref.at[:, pl.ds(0, foreign * HD)], t_ref.at[:, pl.ds(0, foreign * HD)]
        remote(o_all, o_all, out_s.at[0], out_r.at[0], right).wait_recv()
        remote(t_all, t_all, out_s.at[0], out_r.at[1], right).wait_recv()

    pl.when(even)(lambda: drain_parity(3, HEADS - 3))
    pl.when(jnp.logical_not(even))(lambda: drain_parity(4, HEADS - 2))


def shards(queries, keys, values, query_tangent, key_tangent, value_tangent):
    out = jax.ShapeDtypeStruct(queries.shape, jnp.bfloat16)
    bf16, f32 = jnp.bfloat16, jnp.float32
    dma = pltpu.SemaphoreType.DMA
    return pl.pallas_call(
        kernel,
        out_shape=(out, out),
        in_specs=[pl.BlockSpec(memory_space=pl.ANY)] * 6,
        out_specs=(pl.BlockSpec(memory_space=pltpu.VMEM),) * 2,
        scratch_shapes=[
            pltpu.VMEM((6, TOK, HEADS * HD), bf16),
            pltpu.VMEM((HEADS, TOK, 4 * HD), bf16),
            pltpu.VMEM((HEADS, TOK, 2 * HD), bf16),
            pltpu.VMEM((SLOTS, NZ, KEYS, 4 * HD), bf16),
            pltpu.VMEM((SLOTS, QROWS, 2 * HD), bf16),
            pltpu.VMEM((SLOTS, 2, QROWS, HD), bf16),
            pltpu.VMEM((QROWS, HD), f32),
            pltpu.VMEM((QROWS, HD), f32),
            pltpu.VMEM((QROWS, 2 * HD), f32),
            pltpu.VMEM((QROWS, 2 * HD), f32),
            dma((6,)),
            dma((SLOTS,)), dma((SLOTS, NZ)),
            dma((SLOTS,)), dma((SLOTS,)),
            dma((SLOTS,)), dma((SLOTS, NZ, 2)),
            dma((SLOTS,)), dma((SLOTS, NZ)),
            dma((SLOTS,)), dma((SLOTS, NZ)),
            dma((SLOTS,)), dma((2,)),
        ],
        compiler_params=pltpu.CompilerParams(
            collective_id=0, has_side_effects=True, vmem_limit_bytes=48 * 2**20
        ),
        cost_estimate=pl.CostEstimate(flops=8 * 10**9, bytes_accessed=3 * 10**6, transcendentals=5 * 10**6),
    )(queries, keys, values, query_tangent, key_tangent, value_tangent)


def solution(mesh):
    spec = P(("dp", "blk", "uly"), None)
    return jax.shard_map(shards, mesh=mesh, in_specs=(spec,) * 6, out_specs=(spec,) * 2, check_vma=False)
```

time: 522 us -> 94.2 us (0.18)
  waiting for transfers between devices: 236 us -> 0 us
  matrix products: 109 us -> 0 us
  Pallas kernels: 0 us -> 85.9 us
  blocking collectives: 71.2 us -> 0 us
  local copies, waits for them, and re-layouts: 66 us -> 7.28 us
  starting transfers between devices: 16.1 us -> 0 us
  between operations: 14 us -> 0.65 us
    all_gather x4 -> x0, waiting for transfers between devices: 186 us -> none  [the longest x1 59.7 us: shards(): lax.all_gather(kdot_local, 'blk', axis=0, tiled=True)]
    dot_general x60 -> x0, matrix products: 109 us -> none  [the longest x30 55.1 us: scores_of(): jnp.einsum('qd,kd->qk', query_part, key_part, preferred_element_type=jnp....]
    pallas_call x0 -> x1, Pallas kernels: none -> 85.9 us  [shards(): pl.pallas_call(kernel, out_shape=(out, out), in_specs=[pl.BlockSpec(memor...]
    all_to_all x4 -> x0, blocking collectives: 71.2 us -> none  [the longest x1 20.9 us: shards(): lax.all_to_all(keys, 'uly', split_axis=1, concat_axis=0, tiled=True)]
    all_gather x4 -> x0, local copies, waits for them, and re-layouts: 57.3 us -> none  [the longest x1 14.4 us: shards(): lax.all_gather(kdot_local, 'blk', axis=0, tiled=True)]
    all_to_all x4 -> x0, waiting for transfers between devices: 50.1 us -> none  [the longest x1 14.1 us: shards(): lax.all_to_all(query_tangent, 'uly', split_axis=1, concat_axis=0, tiled=T...]
    all_to_all x4 -> x0, starting transfers between devices: 15.9 us -> none  [the longest x1 5.58 us: shards(): lax.all_to_all(output_tok, 'uly', split_axis=0, concat_axis=1, tiled=True)]
    unnamed x8 -> x14, local copies, waits for them, and re-layouts: 0.02 us -> 7.28 us
  transfers between devices with their start and end apart: 8 -> 0, of which waited for: 8 -> 0; matrix products, arithmetic and copies ran while one was open for 9% -> 0% of each run, Pallas kernels for 0% -> 0%
where the time goes in v1:
time: 94.2 us; the launch traced here: 93.8 us
  Pallas kernels  85.9 us (91%)
  local copies, waits for them, and re-layouts  7.28 us (8%)
    pallas_call x1, Pallas kernels, shards(): pl.pallas_call(kernel, out_shape=(out, out), in_specs=[pl.BlockSpec(memor...  85.9 us
    unnamed x14, local copies, waits for them, and re-layouts  7.28 us

profile of v1, /device:TPU:16, one launch (start us, length us, event | category | flops | bytes accessed | tf_op | source)
XLA Modules:
  0.0 93.8 jit_solution(12197585717489563620)
XLA Ops:
  0.6 0.0 copy-start
  0.6 1.0 %copy-done = bf16[64,2560]{1,0:T(8,128)(2,1)S(1)} copy-done((bf16[64,2560]{1,0:T(8,128)(2,1)S(1)}, bf16[64,2560]{1,0:T(8,128)(2,1)}, u32[]{:S(2)}) %copy-start) | copy-done | bytes 327704
  1.6 0.0 copy-start.1
  1.6 1.0 %copy-done.1 = bf16[64,2560]{1,0:T(8,128)(2,1)S(1)} copy-done((bf16[64,2560]{1,0:T(8,128)(2,1)S(1)}, bf16[64,2560]{1,0:T(8,128)(2,1)}, u32[]{:S(2)}) %copy-start.1) | copy-done | bytes 327704
  2.6 0.0 copy-start.2
  2.6 1.0 %copy-done.2 = bf16[64,2560]{1,0:T(8,128)(2,1)S(1)} copy-done((bf16[64,2560]{1,0:T(8,128)(2,1)S(1)}, bf16[64,2560]{1,0:T(8,128)(2,1)}, u32[]{:S(2)}) %copy-start.2) | copy-done | bytes 327704
  3.6 0.0 copy-start.3
  3.6 1.0 %copy-done.3 = bf16[64,2560]{1,0:T(8,128)(2,1)S(1)} copy-done((bf16[64,2560]{1,0:T(8,128)(2,1)S(1)}, bf16[64,2560]{1,0:T(8,128)(2,1)}, u32[]{:S(2)}) %copy-start.3) | copy-done | bytes 327704
  4.5 0.0 copy-start.4
  4.5 1.0 %copy-done.4 = bf16[64,2560]{1,0:T(8,128)(2,1)S(1)} copy-done((bf16[64,2560]{1,0:T(8,128)(2,1)S(1)}, bf16[64,2560]{1,0:T(8,128)(2,1)}, u32[]{:S(2)}) %copy-start.4) | copy-done | bytes 327704
  5.5 0.0 copy-start.5
  5.5 1.0 %copy-done.5 = bf16[64,2560]{1,0:T(8,128)(2,1)S(1)} copy-done((bf16[64,2560]{1,0:T(8,128)(2,1)S(1)}, bf16[64,2560]{1,0:T(8,128)(2,1)}, u32[]{:S(2)}) %copy-start.5) | copy-done | bytes 327704
  6.5 85.9 %shard_map.77 = (bf16[64,2560]{1,0:T(8,128)(2,1)S(1)}, bf16[64,2560]{1,0:T(8,128)(2,1)S(1)}) custom-call(bf16[64,2560]{1,0:T(8,128)(2,1)S(1)} %copy-done, bf16[64,2560]{1,0:T(8,128)(2,1)S(1)} %copy-done.1, bf16[64,2560]{1,0:T(8,128)(2,1)S(1)} %copy-done.2, bf16[64,2560]{1,0:T(8,128)(2,1)S(1)} %copy-done.3, bf16[64,2560]{1,0:T(8,128)(2,1)S(1)} %copy-done.4, ...), custom_call_target="tpu_custom_call" | custom-call | flops 8000000000 | bytes 3000000 | tf_op jit(solution)/shard_map/pallas_call | solution.py:285
  92.4 0.7 copy.10
  93.1 0.7 copy.11
Async XLA Ops:
  0.6 1.0 %copy-start = (bf16[64,2560]{1,0:T(8,128)(2,1)S(1)}, bf16[64,2560]{1,0:T(8,128)(2,1)}, u32[]{:S(2)}) copy-start(bf16[64,2560]{1,0:T(8,128)(2,1)} %q_hbm.1) | copy-start | bytes 983044
  1.6 1.0 %copy-start.1 = (bf16[64,2560]{1,0:T(8,128)(2,1)S(1)}, bf16[64,2560]{1,0:T(8,128)(2,1)}, u32[]{:S(2)}) copy-start(bf16[64,2560]{1,0:T(8,128)(2,1)} %k_hbm.1) | copy-start | bytes 983044
  2.6 1.0 %copy-start.2 = (bf16[64,2560]{1,0:T(8,128)(2,1)S(1)}, bf16[64,2560]{1,0:T(8,128)(2,1)}, u32[]{:S(2)}) copy-start(bf16[64,2560]{1,0:T(8,128)(2,1)} %v_hbm.1) | copy-start | bytes 983044
  3.6 1.0 %copy-start.3 = (bf16[64,2560]{1,0:T(8,128)(2,1)S(1)}, bf16[64,2560]{1,0:T(8,128)(2,1)}, u32[]{:S(2)}) copy-start(bf16[64,2560]{1,0:T(8,128)(2,1)} %qd_hbm.1) | copy-start | bytes 983044
  4.5 1.0 %copy-start.4 = (bf16[64,2560]{1,0:T(8,128)(2,1)S(1)}, bf16[64,2560]{1,0:T(8,128)(2,1)}, u32[]{:S(2)}) copy-start(bf16[64,2560]{1,0:T(8,128)(2,1)} %kd_hbm.1) | copy-start | bytes 983044
  5.5 1.0 %copy-start.5 = (bf16[64,2560]{1,0:T(8,128)(2,1)S(1)}, bf16[64,2560]{1,0:T(8,128)(2,1)}, u32[]{:S(2)}) copy-start(bf16[64,2560]{1,0:T(8,128)(2,1)} %vd_hbm.1) | copy-start | bytes 983044

commit v2 on v1

v2 whole, which is shorter than its diff:
```python
import functools
import math

import jax
import jax.numpy as jnp
from jax import lax
from jax.experimental import pallas as pl
from jax.experimental.pallas import tpu as pltpu
from jax.sharding import PartitionSpec as P

HEADS = 20
HD = 128
TOK = 64
NZ, NX, NC = 8, 4, 2
KEYS = TOK * NX * NC
QROWS = TOK * NZ
SCALE = HD ** -0.5
TO_LOG2 = SCALE * math.log2(math.e)
LAG_X, LAG_RELAY, LAG_RING, LAG_PAIR = 2, 4, 5, 4
LATE = 12
PAIR, RING = 0, 1
NEAR_FIRST = (1, 7, 2, 6, 3, 5, 4)


def dot_t(a, b):
    return lax.dot_general(a, b, (((1,), (1,)), ((), ())), preferred_element_type=jnp.float32)


def dot(a, b):
    return lax.dot_general(a, b, (((1,), (0,)), ((), ())), preferred_element_type=jnp.float32)


def attend(q, kv, m_ref, l_ref, ap_ref, aw_ref):
    s = dot_t(q[:, HD:], kv[:, :HD])
    sd = dot_t(q[:, :], kv[:, : 2 * HD])
    n = s.shape[1]
    best = s[:, :HD]
    for j in range(HD, n, HD):
        best = jnp.maximum(best, s[:, j : j + HD])
    best = jnp.max(best, axis=1, keepdims=True) * TO_LOG2
    m_old = m_ref[...]
    m_new = jnp.maximum(m_old, jnp.broadcast_to(best, m_old.shape))
    alpha = jnp.exp2(m_old - m_new)
    m_ref[...] = m_new
    p = jnp.exp2(s * TO_LOG2 - jnp.concatenate([m_new] * (n // HD), axis=1))
    w = p * sd
    total = p[:, :HD]
    for j in range(HD, n, HD):
        total = total + p[:, j : j + HD]
    v = kv[:, 3 * HD :]
    po = dot(p.astype(jnp.bfloat16), kv[:, 2 * HD :])
    wo = dot(w.astype(jnp.bfloat16), jnp.concatenate([v, jnp.ones_like(v)], axis=1))
    alpha2 = jnp.concatenate([alpha, alpha], axis=1)
    l_ref[...] = l_ref[...] * alpha + total
    ap_ref[...] = ap_ref[...] * alpha2 + po
    aw_ref[...] = aw_ref[...] * alpha2 + wo


def kernel(
    q_hbm, k_hbm, v_hbm, qd_hbm, kd_hbm, vd_hbm, o_ref, t_ref,
    stage, pack_kv, pack_q, kv, qb, ob, m_ref, l_ref, ap_ref, aw_ref,
    load_sem, zkv_s, zkv_r, zq_s, zq_r, in_s, in_r, x_s, x_r, rel_s, rel_r, sib_s, sib_r, out_s, out_r,
):
    blk, uly = lax.axis_index("blk"), lax.axis_index("uly")
    core = lax.rem(blk, NC)
    x = lax.rem(blk // NC, NX)
    z = uly * 4 + blk // (NC * NX)
    even = lax.rem(z, 2) == 0
    outer_x = NX - 1 - x
    inner_x = x + 1 - 2 * lax.rem(x, 2)
    pair, outer_pair = x // 2, outer_x // 2

    def device(zz, xx, cc):
        return {"blk": (lax.rem(zz, 4) * NX + xx) * NC + cc, "uly": zz // 4}

    def z_peer(dz):
        return lax.rem(z + dz, NZ)

    def pair_head(zz, pp):
        return 5 * (zz // 2) + 3 * lax.rem(zz, 2) + pp

    def ring_head(zz):
        return 5 * (zz // 2) + 2

    sibling = device(z, x, 1 - core)
    inner = device(z, inner_x, core)
    right, left = device(z, lax.rem(x + 1, NX), core), device(z, lax.rem(x + 3, NX), core)

    def remote(src, dst, send, recv, to):
        return pltpu.make_async_remote_copy(
            src_ref=src, dst_ref=dst, send_sem=send, recv_sem=recv,
            device_id=to, device_id_type=pl.DeviceIdType.MESH,
        )

    peers = [device(z_peer(dz), x, core) for dz in range(1, NZ)]
    peers += [device(z_peer(dz), outer_x, core) for dz in range(NZ)]
    peers += [inner, sibling]
    barrier = pltpu.get_barrier_semaphore()
    for to in peers:
        pl.semaphore_signal(barrier, inc=1, device_id=to, device_id_type=pl.DeviceIdType.MESH)

    loads = []
    for i, ref in enumerate((k_hbm, kd_hbm, vd_hbm, v_hbm, qd_hbm, q_hbm)):
        copy = pltpu.make_async_copy(ref, stage.at[i], load_sem.at[i])
        copy.start()
        loads.append(copy)

    ring_heads = range(2, HEADS, 5)
    pair_heads = [h for h in range(HEADS) if h not in ring_heads]

    def pack(into, first, count, heads):
        for h in heads:
            for i in range(count):
                into[h, :, i * HD : (i + 1) * HD] = stage[first + i, :, pl.ds(h * HD, HD)]

    def blocks(first, count):
        return pl.ds(first * TOK, count * TOK)

    my_rows = pl.ds(pl.multiple_of(z * TOK, TOK), TOK)

    def send_ring(dz):
        zz = z_peer(dz)
        remote(pack_kv.at[ring_head(zz)], kv.at[RING, z, blocks(0, 1)], zkv_s.at[RING], zkv_r.at[RING, dz],
               device(zz, x, core)).start()

    def send_ring_q(dz):
        zz = z_peer(dz)
        remote(pack_q.at[ring_head(zz)], qb.at[2, my_rows], zq_s.at[2], zq_r.at[2], device(zz, x, core)).start()

    def to_ring(send):
        for dz in NEAR_FIRST:
            pl.when(lax.rem(z + dz, 2) == 0)(functools.partial(send, dz))

    def keep_ring():
        kv[RING, z, blocks(0, 1), :] = pack_kv[ring_head(z)]

    def keep_ring_q():
        qb[2, my_rows, :] = pack_q[ring_head(z)]

    for copy in loads[:4]:
        copy.wait()
    pack(pack_kv, 0, 4, ring_heads)
    pl.when(even)(keep_ring)
    pl.semaphore_wait(barrier, len(peers))
    to_ring(send_ring)

    for copy in loads[4:]:
        copy.wait()
    pack(pack_q, 4, 2, ring_heads)
    pl.when(even)(keep_ring_q)
    to_ring(send_ring_q)

    pack(pack_q, 4, 2, pair_heads)
    qb[0, my_rows, :] = pack_q[pair_head(z, pair)]
    for dz in NEAR_FIRST:
        zz = z_peer(dz)
        remote(pack_q.at[pair_head(zz, pair)], qb.at[0, my_rows], zq_s.at[0], zq_r.at[0],
               device(zz, x, core)).start()

    pack(pack_kv, 0, 4, pair_heads)
    kv[PAIR, z, blocks(0, 1), :] = pack_kv[pair_head(z, pair)]
    for dz in (0,) + NEAR_FIRST:
        zz = z_peer(dz)
        if dz:
            remote(pack_kv.at[pair_head(zz, pair)], kv.at[PAIR, z, blocks(0, 1)], zkv_s.at[PAIR],
                   zkv_r.at[PAIR, dz], device(zz, x, core)).start()
        remote(pack_kv.at[pair_head(zz, outer_pair)], kv.at[PAIR, z, blocks(1, 1)], zkv_s.at[PAIR],
               zkv_r.at[PAIR, dz], device(zz, outer_x, core)).start()

    def send_outer_q():
        for dz in (0,) + NEAR_FIRST:
            zz = z_peer(dz)
            remote(pack_q.at[pair_head(zz, outer_pair)], qb.at[1, my_rows], zq_s.at[1], zq_r.at[1],
                   device(zz, outer_x, core)).start()

    m_ref[...] = jnp.full_like(m_ref, -1e30)
    l_ref[...] = jnp.zeros_like(l_ref)
    ap_ref[...] = jnp.zeros_like(ap_ref)
    aw_ref[...] = jnp.zeros_like(aw_ref)

    def chunk_of(i):
        half = (i + 1) // 2
        dz = jnp.where(lax.rem(i, 2) == 1, half, lax.rem(NZ - half, NZ))
        return dz, lax.rem(z - dz + NZ, NZ)

    def to_sibling(way, i, zz):
        remote(kv.at[way, zz, blocks(0, 4)], kv.at[way, zz, blocks(4, 4)], sib_s.at[way], sib_r.at[way, i],
               sibling).start()

    def pair_arrived(i):
        dz, zz = chunk_of(i)
        one, two = kv.at[PAIR, zz, blocks(1, 1)], kv.at[PAIR, zz, blocks(0, 2)]

        @pl.when(i == 0)
        def _():
            remote(one, one, zkv_s.at[PAIR], zkv_r.at[PAIR, dz], inner).wait_recv()

        @pl.when(i > 0)
        def _():
            remote(two, two, zkv_s.at[PAIR], zkv_r.at[PAIR, dz], inner).wait_recv()

        remote(two, kv.at[PAIR, zz, blocks(2, 2)], in_s, in_r.at[i], inner).start()

    def pair_from_inner(i):
        dz, zz = chunk_of(i)
        two = kv.at[PAIR, zz, blocks(2, 2)]
        remote(two, two, in_s, in_r.at[i], inner).wait_recv()
        to_sibling(PAIR, i, zz)

    def ring_arrived(i):
        dz, zz = chunk_of(i)
        own = kv.at[RING, zz, blocks(0, 1)]

        @pl.when(i > 0)
        def _():
            remote(own, own, zkv_s.at[RING], zkv_r.at[RING, dz], right).wait_recv()

        remote(own, kv.at[RING, zz, blocks(1, 1)], x_s, x_r.at[i, 0], right).start()
        remote(own, kv.at[RING, zz, blocks(2, 1)], x_s, x_r.at[i, 1], left).start()

    def ring_from_x(i):
        dz, zz = chunk_of(i)
        from_left, from_right, far = (kv.at[RING, zz, blocks(b, 1)] for b in (1, 2, 3))
        remote(from_left, from_left, x_s, x_r.at[i, 0], right).wait_recv()
        remote(from_right, from_right, x_s, x_r.at[i, 1], left).wait_recv()
        pl.when(core == 0)(lambda: remote(from_left, far, rel_s, rel_r.at[i], right).start())
        pl.when(core == 1)(lambda: remote(from_right, far, rel_s, rel_r.at[i], left).start())

    def ring_from_relay(i):
        dz, zz = chunk_of(i)
        far = kv.at[RING, zz, blocks(3, 1)]
        remote(far, far, rel_s, rel_r.at[i], right).wait_recv()
        to_sibling(RING, i, zz)

    def finish(group, head):
        inv = 1.0 / jnp.sum(l_ref[group], axis=1, keepdims=True)
        o = ap_ref[group, :, HD:] * inv
        tilt = aw_ref[group, :, HD:] * (SCALE * inv)
        tangent = (ap_ref[group, :, :HD] + aw_ref[group, :, :HD] * SCALE) * inv - o * tilt
        ob[group, 0] = o.astype(jnp.bfloat16)
        ob[group, 1] = tangent.astype(jnp.bfloat16)
        columns = pl.ds(pl.multiple_of(head * HD, HD), HD)
        to_x = outer_x if group == 1 else x
        if group != 1:
            o_ref[:, columns] = ob[group, 0, my_rows, :]
            t_ref[:, columns] = ob[group, 1, my_rows, :]
        for dz in reversed(NEAR_FIRST + ((0,) if group == 1 else ())):
            to_z = z_peer(dz)
            rows = pl.ds(pl.multiple_of(to_z * TOK, TOK), TOK)
            to = device(to_z, to_x, core)
            remote(ob.at[group, 0, rows], o_ref.at[:, columns], out_s.at[group], out_r.at[0], to).start()
            remote(ob.at[group, 1, rows], t_ref.at[:, columns], out_s.at[group], out_r.at[1], to).start()

    def from_sibling(way, i):
        other = kv.at[way, 0, blocks(4, 4)]
        remote(other, other, sib_s.at[way], sib_r.at[way, i], sibling).wait_recv()

    def add_chunk(group, way, i):
        dz, zz = chunk_of(i)
        attend(qb.at[group], kv.at[way, zz], m_ref.at[group], l_ref.at[group], ap_ref.at[group], aw_ref.at[group])

    seven = qb.at[0, pl.ds(0, QROWS - TOK)]

    def ring_compute(i):
        from_sibling(RING, i)

        @pl.when(i == 0)
        def _():
            remote(seven, seven, zq_s.at[2], zq_r.at[2], inner).wait_recv()

        add_chunk(2, RING, i)
        pl.when(i == NZ - 1)(lambda: finish(2, ring_head(z)))

    def pair_compute(i):
        from_sibling(PAIR, i)

        @pl.when(i == 0)
        def _():
            remote(seven, seven, zq_s.at[0], zq_r.at[0], inner).wait_recv()

        add_chunk(0, PAIR, i)
        pl.when(i == NZ - 1)(lambda: finish(0, pair_head(z, pair)))

    first = jnp.where(even, 0, NZ)

    def step(n, carry):
        pl.when(n == LATE)(send_outer_q)
        for ring_lag, ring_do, pair_lag, pair_do in (
            (0, ring_arrived, 0, pair_arrived),
            (LAG_X, ring_from_x, LAG_X, pair_from_inner),
            (LAG_RELAY, ring_from_relay, None, None),
            (LAG_RING, ring_compute, LAG_PAIR, pair_compute),
        ):
            k = n - ring_lag
            pl.when(jnp.logical_and(k >= first, k < NZ))(functools.partial(ring_do, k))
            if pair_do is not None:
                k = n - pair_lag
                pl.when(jnp.logical_and(k >= NZ, k < 2 * NZ))(functools.partial(pair_do, k - NZ))
        return carry

    lax.fori_loop(first, 2 * NZ + LAG_PAIR, step, 0)

    remote(qb.at[1], qb.at[1], zq_s.at[1], zq_r.at[1], inner).wait_recv()

    def outer_compute(i, carry):
        add_chunk(1, PAIR, i)
        return carry

    lax.fori_loop(0, NZ, outer_compute, 0)
    finish(1, pair_head(z, pair))

    def sent(ref, sem):
        remote(ref, ref, sem, rel_r.at[0], inner).wait_send()

    def arrived(ref, sem):
        remote(ref, ref, load_sem.at[0], sem, inner).wait_recv()

    sent(pack_q.at[pl.ds(0, NZ - 1)], zq_s.at[0])
    sent(pack_q.at[pl.ds(0, NZ)], zq_s.at[1])
    sent(pack_kv.at[pl.ds(0, 2 * NZ - 1)], zkv_s.at[PAIR])
    sent(kv.at[PAIR, pl.ds(0, 2)], in_s)
    sent(kv.at[PAIR, pl.ds(0, 4)], sib_s.at[PAIR])
    sent(ob.at[0, :, pl.ds(0, QROWS - TOK)], out_s.at[0])
    sent(ob.at[1], out_s.at[1])

    def by_parity(targets, foreign):
        sent(pack_kv.at[pl.ds(0, targets)], zkv_s.at[RING])
        sent(pack_q.at[pl.ds(0, targets)], zq_s.at[2])
        arrived(o_ref.at[:, pl.ds(0, foreign * HD)], out_r.at[0])
        arrived(t_ref.at[:, pl.ds(0, foreign * HD)], out_r.at[1])

    @pl.when(even)
    def _():
        sent(kv.at[RING, pl.ds(0, 2)], x_s)
        sent(kv.at[RING, 0], rel_s)
        sent(kv.at[RING, pl.ds(0, 4)], sib_s.at[RING])
        sent(ob.at[2, :, pl.ds(0, QROWS - TOK)], out_s.at[2])
        by_parity(NZ // 2 - 1, HEADS - 2)

    pl.when(jnp.logical_not(even))(lambda: by_parity(NZ // 2, HEADS - 1))


def shards(queries, keys, values, query_tangent, key_tangent, value_tangent):
    out = jax.ShapeDtypeStruct(queries.shape, jnp.bfloat16)
    bf16, f32 = jnp.bfloat16, jnp.float32
    dma = pltpu.SemaphoreType.DMA
    return pl.pallas_call(
        kernel,
        out_shape=(out, out),
        in_specs=[pl.BlockSpec(memory_space=pl.ANY)] * 6,
        out_specs=(pl.BlockSpec(memory_space=pltpu.VMEM),) * 2,
        scratch_shapes=[
            pltpu.VMEM((6, TOK, HEADS * HD), bf16),
            pltpu.VMEM((HEADS, TOK, 4 * HD), bf16),
            pltpu.VMEM((HEADS, TOK, 2 * HD), bf16),
            pltpu.VMEM((2, NZ, KEYS, 4 * HD), bf16),
            pltpu.VMEM((3, QROWS, 2 * HD), bf16),
            pltpu.VMEM((3, 2, QROWS, HD), bf16),
            pltpu.VMEM((3, QROWS, HD), f32),
            pltpu.VMEM((3, QROWS, HD), f32),
            pltpu.VMEM((3, QROWS, 2 * HD), f32),
            pltpu.VMEM((3, QROWS, 2 * HD), f32),
            dma((6,)),
            dma((2,)), dma((2, NZ)),
            dma((3,)), dma((3,)),
            dma, dma((NZ,)),
            dma, dma((NZ, 2)),
            dma, dma((NZ,)),
            dma((2,)), dma((2, NZ)),
            dma((3,)), dma((2,)),
        ],
        compiler_params=pltpu.CompilerParams(
            collective_id=0, has_side_effects=True, vmem_limit_bytes=56 * 2**20
        ),
        cost_estimate=pl.CostEstimate(flops=8 * 10**9, bytes_accessed=3 * 10**6, transcendentals=5 * 10**6),
    )(queries, keys, values, query_tangent, key_tangent, value_tangent)


def solution(mesh):
    spec = P(("dp", "blk", "uly"), None)
    return jax.shard_map(shards, mesh=mesh, in_specs=(spec,) * 6, out_specs=(spec,) * 2, check_vma=False)
```

time: 94.2 us -> 87.7 us (0.931)
  local copies, waits for them, and re-layouts: 7.28 us -> 2.49 us
  Pallas kernels: 85.9 us -> 84.2 us
    unnamed x14 -> x4, local copies, waits for them, and re-layouts: 7.28 us -> 2.49 us
    pallas_call x1, Pallas kernels: 85.9 us -> 84.2 us  [shards(): pl.pallas_call(kernel, out_shape=(out, out), in_specs=[pl.BlockSpec(memor...]
where the time goes in v2:
time: 87.7 us; the launch traced here: 87.3 us
  Pallas kernels  84.2 us (96%)
  local copies, waits for them, and re-layouts  2.49 us (3%)
    pallas_call x1, Pallas kernels, shards(): pl.pallas_call(kernel, out_shape=(out, out), in_specs=[pl.BlockSpec(memor...  84.2 us
    unnamed x4, local copies, waits for them, and re-layouts  2.49 us

profile of v2, /device:TPU:16, one launch (start us, length us, event | category | flops | bytes accessed | tf_op | source)
XLA Modules:
  0.0 87.3 jit_solution(7236025454143761044)
XLA Ops:
  0.6 84.2 %shard_map.77 = (bf16[64,2560]{1,0:T(8,128)(2,1)}, bf16[64,2560]{1,0:T(8,128)(2,1)}) custom-call(bf16[64,2560]{1,0:T(8,128)(2,1)} %q_hbm.1, bf16[64,2560]{1,0:T(8,128)(2,1)} %k_hbm.1, bf16[64,2560]{1,0:T(8,128)(2,1)} %v_hbm.1, bf16[64,2560]{1,0:T(8,128)(2,1)} %qd_hbm.1, bf16[64,2560]{1,0:T(8,128)(2,1)} %kd_hbm.1, bf16[64,2560]{1,0:T(8,128)(2,1)} %vd_hbm.1), custom_call_target="tpu_custom_call" | custom-call | flops 8000000000 | bytes 3000000 | tf_op jit(solution)/shard_map/pallas_call | solution.py:347
  84.8 0.0 copy-start
  84.8 1.8 %copy.10 = bf16[64,2560]{1,0:T(8,128)(2,1)} copy(bf16[64,2560]{1,0:T(8,128)(2,1)} %get-tuple-element.4) | data formatting | bytes 655360
  86.6 0.0 copy-done
  86.6 0.7 copy.11
Async XLA Ops:
  84.8 1.8 %copy-start = (bf16[64,2560]{1,0:T(8,128)(2,1)S(1)}, bf16[64,2560]{1,0:T(8,128)(2,1)}, u32[]{:S(2)}) copy-start(bf16[64,2560]{1,0:T(8,128)(2,1)} %get-tuple-element.5) | copy-start | bytes 983044

commit v3 on v2

--- a/solution.py
+++ b/solution.py
@@ -16,8 +16,8 @@
 QROWS = TOK * NZ
 SCALE = HD ** -0.5
 TO_LOG2 = SCALE * math.log2(math.e)
-LAG_X, LAG_RELAY, LAG_RING, LAG_PAIR = 2, 4, 5, 4
-LATE = 12
+LAG_X, LAG_RELAY, LAG_RING, LAG_PAIR = 2, 4, 5, 5
+LATE = 14
 PAIR, RING = 0, 1
 NEAR_FIRST = (1, 7, 2, 6, 3, 5, 4)
 
@@ -150,13 +150,6 @@
     pl.when(even)(keep_ring_q)
     to_ring(send_ring_q)
 
-    pack(pack_q, 4, 2, pair_heads)
-    qb[0, my_rows, :] = pack_q[pair_head(z, pair)]
-    for dz in NEAR_FIRST:
-        zz = z_peer(dz)
-        remote(pack_q.at[pair_head(zz, pair)], qb.at[0, my_rows], zq_s.at[0], zq_r.at[0],
-               device(zz, x, core)).start()
-
     pack(pack_kv, 0, 4, pair_heads)
     kv[PAIR, z, blocks(0, 1), :] = pack_kv[pair_head(z, pair)]
     for dz in (0,) + NEAR_FIRST:
@@ -166,6 +159,13 @@
                    zkv_r.at[PAIR, dz], device(zz, x, core)).start()
         remote(pack_kv.at[pair_head(zz, outer_pair)], kv.at[PAIR, z, blocks(1, 1)], zkv_s.at[PAIR],
                zkv_r.at[PAIR, dz], device(zz, outer_x, core)).start()
+
+    pack(pack_q, 4, 2, pair_heads)
+    qb[0, my_rows, :] = pack_q[pair_head(z, pair)]
+    for dz in NEAR_FIRST:
+        zz = z_peer(dz)
+        remote(pack_q.at[pair_head(zz, pair)], qb.at[0, my_rows], zq_s.at[0], zq_r.at[0],
+               device(zz, x, core)).start()
 
     def send_outer_q():
         for dz in (0,) + NEAR_FIRST:
@@ -370,7 +370,7 @@
             dma((3,)), dma((2,)),
         ],
         compiler_params=pltpu.CompilerParams(
-            collective_id=0, has_side_effects=True, vmem_limit_bytes=56 * 2**20
+            collective_id=0, has_side_effects=True, vmem_limit_bytes=213 * 2**18
         ),
         cost_estimate=pl.CostEstimate(flops=8 * 10**9, bytes_accessed=3 * 10**6, transcendentals=5 * 10**6),
     )(queries, keys, values, query_tangent, key_tangent, value_tangent)

time: 87.7 us -> 83.9 us (0.957)
  Pallas kernels: 84.2 us -> 81.2 us
  local copies, waits for them, and re-layouts: 2.49 us -> 1.45 us
    pallas_call x1, Pallas kernels: 84.2 us -> 81.2 us  [shards(): pl.pallas_call(kernel, out_shape=(out, out), in_specs=[pl.BlockSpec(memor...]
    unnamed x4 -> x2, local copies, waits for them, and re-layouts: 2.49 us -> 1.45 us
where the time goes in v3:
time: 83.9 us; the launch traced here: 83.3 us
  Pallas kernels  81.2 us (97%)
  local copies, waits for them, and re-layouts  1.45 us (2%)
    pallas_call x1, Pallas kernels, shards(): pl.pallas_call(kernel, out_shape=(out, out), in_specs=[pl.BlockSpec(memor...  81.2 us

profile of v3, /device:TPU:16, one launch (start us, length us, event | category | flops | bytes accessed | tf_op | source)
XLA Modules:
  0.0 83.3 jit_solution(15185285247318679850)
XLA Ops:
  0.6 81.2 %shard_map.77 = (bf16[64,2560]{1,0:T(8,128)(2,1)S(1)}, bf16[64,2560]{1,0:T(8,128)(2,1)S(1)}) custom-call(bf16[64,2560]{1,0:T(8,128)(2,1)} %q_hbm.1, bf16[64,2560]{1,0:T(8,128)(2,1)} %k_hbm.1, bf16[64,2560]{1,0:T(8,128)(2,1)} %v_hbm.1, bf16[64,2560]{1,0:T(8,128)(2,1)} %qd_hbm.1, bf16[64,2560]{1,0:T(8,128)(2,1)} %kd_hbm.1, bf16[64,2560]{1,0:T(8,128)(2,1)} %vd_hbm.1), custom_call_target="tpu_custom_call" | custom-call | flops 8000000000 | bytes 3000000 | tf_op jit(solution)/shard_map/pallas_call | solution.py:347
  81.8 0.7 copy.10
  82.6 0.7 copy.11

commit v4 on v3

--- a/solution.py
+++ b/solution.py
@@ -303,10 +303,11 @@
     remote(qb.at[1], qb.at[1], zq_s.at[1], zq_r.at[1], inner).wait_recv()
 
     def outer_compute(i, carry):
-        add_chunk(1, PAIR, i)
+        add_chunk(1, PAIR, 2 * i)
+        add_chunk(1, PAIR, 2 * i + 1)
         return carry
 
-    lax.fori_loop(0, NZ, outer_compute, 0)
+    lax.fori_loop(0, NZ // 2, outer_compute, 0)
     finish(1, pair_head(z, pair))
 
     def sent(ref, sem):

time: 83.9 us -> 83.1 us (level)
  no operation moved by 1% of the time
where the time goes in v4:
time: 83.1 us; the launch traced here: 82.5 us
  Pallas kernels  80.5 us (97%)
  local copies, waits for them, and re-layouts  1.45 us (2%)
    pallas_call x1, Pallas kernels, shards(): pl.pallas_call(kernel, out_shape=(out, out), in_specs=[pl.BlockSpec(memor...  80.5 us

profile of v4, /device:TPU:16, one launch (start us, length us, event | category | flops | bytes accessed | tf_op | source)
XLA Modules:
  0.0 82.5 jit_solution(15060992966253356366)
XLA Ops:
  0.6 80.5 %shard_map.77 = (bf16[64,2560]{1,0:T(8,128)(2,1)S(1)}, bf16[64,2560]{1,0:T(8,128)(2,1)S(1)}) custom-call(bf16[64,2560]{1,0:T(8,128)(2,1)} %q_hbm.1, bf16[64,2560]{1,0:T(8,128)(2,1)} %k_hbm.1, bf16[64,2560]{1,0:T(8,128)(2,1)} %v_hbm.1, bf16[64,2560]{1,0:T(8,128)(2,1)} %qd_hbm.1, bf16[64,2560]{1,0:T(8,128)(2,1)} %kd_hbm.1, bf16[64,2560]{1,0:T(8,128)(2,1)} %vd_hbm.1), custom_call_target="tpu_custom_call" | custom-call | flops 8000000000 | bytes 3000000 | tf_op jit(solution)/shard_map/pallas_call | solution.py:348
  81.1 0.7 copy.10
  81.8 0.7 copy.11
